TPU v7x, 32 devices: a whole 2x2x4 slice. The times are simulated.
32 devices in a mesh: parts: 2 (over x), role: 2 (over core), shard: 8 (over z, y).
Axes of the slice: x: 2, y: 2, z: 4, core: 2. Of those that a mesh axis runs over, the one named last changes fastest.
Arguments:
- states: bfloat16 [4096, 7168], P(('parts', 'shard')), parts along dimension 0, may hold values from -6 to 6
- w_latent: bfloat16 [7168, 512], P('role'), may hold values from -0.0625 to 0.0625
- w_rope: bfloat16 [7168, 64], P('role'), may hold values from -0.0625 to 0.0625
- latent_gain: bfloat16 [512], replicated, may hold values from 0.25 to 1.75
- span_len: int32 [16, 4], P('parts'), parts along dimension 0, may hold values from 1 to 128, 256 in all within a row
- cache_len: int32 [16, 4], P('parts'), parts along dimension 0, may hold values from 1 to 256
- dest: int32 [16, 4], P('parts'), parts along dimension 0, may hold values from 0 to 7, all different within a row; in each aligned block of 8 rows (0 to 7, 8 to 15, ...) at most 8 rows name the same one
- page_table: int32 [16, 24], P(('parts', 'shard')), parts along dimension 0, may hold values from 0 to 23, each once within a row
- latent_pool: bfloat16 [384, 128, 512], P(('parts', 'shard')), parts along dimension 0, may hold values from -6 to 6
- rope_pool: bfloat16 [384, 64, 128], P(('parts', 'shard')), parts along dimension 0, may hold values from -6 to 6
- new_keys: bfloat16 [16, 8, 4, 576], P(('parts', 'shard')), parts along dimension 0, may hold values from -6 to 6
- q_nope: bfloat16 [4, 64, 16384], P(None, 'parts', 'shard'), parts along dimension 1, may hold values from -6 to 6
- q_rope: bfloat16 [4, 64, 8192], P(None, 'parts', 'shard'), parts along dimension 1, may hold values from -64 to 64
- w_uk: bfloat16 [128, 128, 512], P('shard'), may hold values from -0.5 to 0.5
- w_uv: bfloat16 [128, 512, 128], P('shard'), may hold values from -0.25 to 0.25
Outputs:
- head_outputs: bfloat16 [64, 4, 16384], P(('parts', 'role'), None, 'shard'), parts along dimension 0
There are 2 independent parts, one for each index of `parts`. A program takes and returns all parts, laid end to end along the dimension named above; an argument that names none is the same for every part. Nothing has to cross between parts.
Inputs may be any that keep to these rules, and one draw needn't show every extreme that they name: `dest`: A prefill rank's 4 requests go to distinct decode ranks; at most 8 requests of a group go to one decode rank, and some rank receives exactly 8; every rank receives at least one. `span_len`: the 4 lengths of a prefill rank sum to 256; the largest of each rank is 128. `page_table`: each row is a permutation of 0 to 23.
All inputs are finite; a program needn't handle non-finite values.
Results may differ from a plain program's by a relative error of at most 0.0074.
Values may be sent and summed in bfloat16 or wider, within the bound.
A program may use at most 128 MiB of HBM per device.

v0:
```python
import functools

import jax
import jax.numpy as jnp
from jax import lax
from jax.experimental import pallas as pl
from jax.experimental.pallas import tpu as pltpu
from jax.sharding import PartitionSpec as P

MESH = pl.DeviceIdType.MESH
CHUNK = 512
LOW = -1e30
LAST = (((1,), (1,)), ((), ()))


def dot(a, b):
    return jnp.dot(a, b, preferred_element_type=jnp.float32)


def dot_last(a, b):
    return lax.dot_general(a, b, LAST, preferred_element_type=jnp.float32)


def iota(shape, axis):
    return lax.broadcasted_iota(jnp.int32, shape, axis)


def one_hot(hit):
    return jnp.where(hit, 1.0, 0.0).astype(jnp.bfloat16)


def kernel(
    dims,
    dest_ref,
    cache_ref,
    span_ref,
    table_ref,
    gain_ref,
    frequency_ref,
    states_hbm,
    w_latent_hbm,
    w_rope_hbm,
    pool_hbm,
    rope_pool_hbm,
    new_latent_hbm,
    new_rope_hbm,
    nope_hbm,
    rotary_hbm,
    uk_hbm,
    uv_hbm,
    out_ref,
    states,
    w_latent,
    w_rope,
    pool,
    rope_pool,
    new_latent,
    new_rope,
    nope,
    uk,
    uv,
    slots,
    k_send,
    k_got,
    r_send,
    r_got,
    q_send,
    q_got,
    rotary_got,
    rotary_rows,
    part_latent,
    part_rope,
    there_latent,
    there_rope,
    span_latent,
    span_rope,
    mine_latent,
    mine_rope,
    other_latent,
    other_rope,
    attended,
    back,
    give,
    taken,
    load_sem,
    k_sem,
    r_sem,
    q_sem,
    rot_sem,
    part_sem,
    page_sem,
    back_sem,
    give_sem,
):
    shards, requests, steps, heads, scale, pages_each = dims
    role = lax.axis_index("role")
    me = lax.axis_index("shard")
    bf16 = jnp.bfloat16
    page_rows, width = pool.shape[1:]
    rope_width = w_rope.shape[1]
    depth = w_latent.shape[0]
    head_width = uk.shape[0] // heads
    value_width = uv.shape[2]
    tokens = states.shape[0]
    each = steps * heads
    query_rows = requests * each
    half = shards // 2
    pair_rows = requests * steps

    loads = [
        (pool_hbm, pool),
        (rope_pool_hbm, rope_pool),
        (new_latent_hbm, new_latent),
        (new_rope_hbm, new_rope),
        (nope_hbm.at[:, pl.ds(pl.multiple_of(role * nope.shape[1], 128), nope.shape[1])], nope),
        (uk_hbm.at[pl.ds(pl.multiple_of(role * uk.shape[0], 128), uk.shape[0])], uk),
        (states_hbm.at[:, pl.ds(pl.multiple_of(role * depth, 128), depth)], states),
        (w_latent_hbm, w_latent),
        (w_rope_hbm, w_rope),
        (uv_hbm.at[pl.ds(role * heads, heads)], uv),
        (
            rotary_hbm.at[
                me, :, pl.ds(pl.multiple_of(role * rotary_got.shape[2], 128), rotary_got.shape[2])
            ],
            rotary_got.at[me],
        ),
    ]
    loads = [pltpu.make_async_copy(a, b, load_sem.at[i]) for i, (a, b) in enumerate(loads)]
    for load in loads:
        load.start()

    barrier = pltpu.get_barrier_semaphore()
    for step in range(1, shards):
        peer = lax.rem(me + step, shards)
        pl.semaphore_signal(barrier, inc=1, device_id={"shard": peer}, device_id_type=MESH)
    pl.semaphore_signal(barrier, inc=1, device_id={"role": 1 - role}, device_id_type=MESH)

    def to_shard(source, target, sem, step, peer):
        return pltpu.make_async_remote_copy(
            src_ref=source,
            dst_ref=target,
            send_sem=sem.at[(0,) + step],
            recv_sem=sem.at[(1,) + step],
            device_id={"shard": peer},
            device_id_type=MESH,
        )

    def to_role(source, target, sem, step):
        return pltpu.make_async_remote_copy(
            src_ref=source,
            dst_ref=target,
            send_sem=sem.at[0, step],
            recv_sem=sem.at[1, step],
            device_id={"role": 1 - role},
            device_id_type=MESH,
        )

    def find(p, count):
        slot = jnp.int32(0)
        for j in range(requests):
            hit = dest_ref[p, j] == me
            slot = jnp.where(hit, count, slot)
            count = count + jnp.where(hit, 1, 0)
        slots[p] = jnp.minimum(slot, new_latent.shape[0] - 1)
        return count

    lax.fori_loop(0, shards, find, jnp.int32(0))
    for load in loads[:4]:
        load.wait()
    pl.semaphore_wait(barrier, shards)

    def k_copy(step, peer, slot):
        return to_shard(k_send.at[peer], k_got.at[slot], k_sem, (step,), peer)

    def r_copy(step, peer, slot):
        return to_shard(r_send.at[peer], r_got.at[slot], r_sem, (step,), peer)

    def q_copy(step, peer, slot):
        return to_shard(q_send.at[peer], q_got.at[slot], q_sem, (step,), peer)

    def rot_copy(step, peer, slot):
        lanes = rotary_got.shape[2]
        source = rotary_hbm.at[peer, :, pl.ds(pl.multiple_of(role * lanes, 128), lanes)]
        return to_shard(source, rotary_got.at[slot], rot_sem, (step,), peer)

    def fill_pages(latent_to, rope_to, peer):
        slot = slots[peer]
        page = table_ref[0, slot * pages_each + role]
        latent_to[:page_rows] = pool[page]
        latent_to[page_rows:] = new_latent[slot]
        rope_to[:rope_width] = rope_pool[page]
        rope_to[rope_width:] = new_rope[slot]

    def send_pages(step, carry):
        peer = lax.rem(me + step, shards)
        fill_pages(k_send.at[peer], r_send.at[peer], peer)
        k_copy(step, peer, me).start()
        r_copy(step, peer, me).start()
        return carry

    lax.fori_loop(1, shards, send_pages, 0)
    for load in loads[4:6]:
        load.wait()

    spread = one_hot(
        lax.div(iota((query_rows, pair_rows), 0), heads) == iota((query_rows, pair_rows), 1)
    )
    shape = (query_rows, heads * head_width)
    own_lanes = lax.div(iota(shape, 1), head_width) == lax.rem(iota(shape, 0), heads)

    def absorb(peer):
        rows = nope[pl.ds(pl.multiple_of(peer * pair_rows, 16), pair_rows), :]
        wide = jnp.where(own_lanes, dot(spread, rows), 0.0).astype(bf16)
        return dot(wide, uk[...]).astype(bf16).reshape(requests, each, width)

    def send_queries(step, carry):
        peer = lax.rem(me + step, shards)
        q_send[peer] = absorb(peer)
        q_copy(step, peer, me).start()
        rot_copy(step, peer, me).start()
        return carry

    lax.fori_loop(1, shards, send_queries, 0)
    q_got[me] = absorb(me)
    fill_pages(k_got.at[me], r_got.at[me], me)

    for load in loads[6:9]:
        load.wait()
    part_latent[...] = jnp.zeros_like(part_latent)
    part_rope[...] = jnp.zeros_like(part_rope)

    def project(k, carry):
        where = pl.ds(pl.multiple_of(k * CHUNK, CHUNK), CHUNK)
        rows = states[:, where]
        part_latent[...] += dot(rows, w_latent[where, :])
        part_rope[...] += dot(rows, w_rope[where, :])
        return carry

    lax.fori_loop(0, depth // CHUNK, project, 0)
    parts = [
        to_role(part_latent, there_latent, part_sem, 0),
        to_role(part_rope, there_rope, part_sem, 1),
    ]
    for copy in parts:
        copy.start()
    position = iota((tokens, 1), 0)
    row = position
    ends = jnp.int32(0)
    for j in range(requests):
        begin = ends
        ends = ends + span_ref[me, j]
        inside = (row >= begin) & (row < ends)
        position = position + jnp.where(inside, cache_ref[me, j] - begin, 0)
    angle = position.astype(jnp.float32) * frequency_ref[...]
    first = iota((tokens, rope_width), 1) < rope_width // 2
    cosine = jnp.cos(angle)
    sine = jnp.sin(angle)
    sine = jnp.where(first, -sine, sine)
    for copy in parts:
        copy.wait()
    raw = part_latent[...] + there_latent[...]
    mean_square = jnp.sum(raw * raw, axis=1, keepdims=True) * (1.0 / width)
    span_latent[...] = (
        raw * lax.rsqrt(mean_square + 1e-06) * gain_ref[...].astype(jnp.float32)
    ).astype(bf16)
    raw = part_rope[...] + there_rope[...]
    turned = jnp.concatenate([raw[:, rope_width // 2 :], raw[:, : rope_width // 2]], axis=1)
    span_rope[...] = (raw * cosine + turned * sine).astype(bf16)

    def take_pages(step, carry):
        origin = lax.rem(me + shards - step, shards)
        k_copy(step, origin, origin).wait_recv()
        r_copy(step, origin, origin).wait_recv()
        return carry

    lax.fori_loop(1, shards, take_pages, 0)
    page_copies = []
    for j in range(requests):
        mine_latent[j] = k_got[dest_ref[me, j]]
        mine_rope[j] = r_got[dest_ref[me, j]]
    for j in range(requests):
        page_copies.append(
            to_role(mine_latent.at[j, pl.ds(0, page_rows)], other_latent.at[j], page_sem, 2 * j)
        )
        page_copies.append(
            to_role(mine_rope.at[j, pl.ds(0, rope_width)], other_rope.at[j], page_sem, 2 * j + 1)
        )
    for copy in page_copies:
        copy.start()

    loads[10].wait()
    lanes = heads * rope_width
    own_rope = lax.div(iota((query_rows, lanes), 1), rope_width) == lax.rem(
        iota((query_rows, lanes), 0), heads
    )
    fold = one_hot(
        lax.rem(iota((lanes, rope_width), 0), rope_width) == iota((lanes, rope_width), 1)
    )

    def unfold(origin):
        wide = jnp.where(own_rope, dot(spread, rotary_got[origin]), 0.0).astype(bf16)
        rotary_rows[origin] = dot(wide, fold).astype(bf16).reshape(requests, each, rope_width)

    unfold(me)

    def take_queries(step, carry):
        origin = lax.rem(me + shards - step, shards)
        rot_copy(step, origin, origin).wait_recv()
        unfold(origin)
        q_copy(step, origin, origin).wait_recv()
        return carry

    lax.fori_loop(1, shards, take_queries, 0)
    for copy in page_copies:
        copy.wait()

    rows = shards * each

    def back_copy(j, step, peer, slot):
        return to_shard(attended.at[j, peer], back.at[slot, j], back_sem, (j, step), peer)

    def attend(j, carry):
        begin = jnp.int32(0)
        for i in range(requests):
            begin = begin + jnp.where(i < j, span_ref[me, i], 0)
        end = begin + span_ref[me, j]
        cached = cache_ref[me, j]
        ql = q_got[:, j].reshape(rows, width)
        qr = rotary_rows[:, j].reshape(rows, rope_width)
        mine = mine_latent[j, :page_rows]
        fresh = mine_latent[j, page_rows:]
        fresh_rope = mine_rope[j, rope_width:, :rope_width]
        other = other_latent[j]
        page_column = iota((rows, page_rows), 1)
        span_column = iota((rows, tokens), 1)
        count = fresh.shape[0]
        time = lax.div(lax.rem(iota((rows, count), 0), each), heads)
        groups = (
            (
                dot_last(ql, mine) + dot(qr, mine_rope[j, :rope_width]),
                page_column + role * page_rows < cached,
                mine,
            ),
            (
                dot_last(ql, other) + dot(qr, other_rope[j]),
                page_column + (1 - role) * page_rows < cached,
                other,
            ),
            (
                dot_last(ql, span_latent[...]) + dot_last(qr, span_rope[...]),
                (span_column >= begin) & (span_column < end),
                span_latent[...],
            ),
            (
                dot_last(ql, fresh) + dot_last(qr, fresh_rope),
                iota((rows, count), 1) <= time,
                fresh,
            ),
        )
        scores = [jnp.where(live, score * scale, LOW) for score, live, _ in groups]
        peak = jnp.max(scores[0], axis=1, keepdims=True)
        for score in scores[1:]:
            peak = jnp.maximum(peak, jnp.max(score, axis=1, keepdims=True))
        total = jnp.zeros((rows, 1), jnp.float32)
        weighted = jnp.zeros((rows, width), jnp.float32)
        for score, (_, live, keys) in zip(scores, groups):
            weight = jnp.where(live, jnp.exp(score - peak), 0.0)
            total = total + jnp.sum(weight, axis=1, keepdims=True)
            weighted = weighted + dot(weight.astype(bf16), keys)
        attended[j] = (weighted / total).astype(bf16).reshape(shards, each, width)

        def send(step, inner):
            peer = lax.rem(me + step, shards)
            back_copy(j, step, peer, me).start()
            return inner

        lax.fori_loop(1, shards, send, 0)
        back[me, j] = attended[j, me]
        return carry

    lax.fori_loop(0, requests, attend, 0)
    loads[9].wait()

    def arrived(p):
        step = lax.rem(me - p + shards, shards)

        @pl.when(step > 0)
        def _():
            for j in range(requests):
                back_copy(j, step, p, p).wait_recv()

    def values(p, h):
        own = back[p].reshape(query_rows, width)
        pick = one_hot(
            iota((pair_rows, query_rows), 1) == iota((pair_rows, query_rows), 0) * heads + h
        )
        return dot(pick, dot(own, uv[h]).astype(bf16)).astype(bf16)

    def give_copy(i):
        return to_role(give.at[i], taken.at[i], give_sem, i)

    def give_rows(i, carry):
        p = (1 - role) * half + i
        arrived(p)
        for h in range(heads):
            give[i, :, h * value_width : (h + 1) * value_width] = values(p, h)
        give_copy(i).start()
        return carry

    lax.fori_loop(0, half, give_rows, 0)
    out_lanes = heads * value_width

    def keep_rows(i, carry):
        p = role * half + i
        arrived(p)
        for h in range(heads):
            lane = pl.multiple_of(role * out_lanes + h * value_width, 128)
            out_ref[pl.ds(pl.multiple_of(i * pair_rows, 16), pair_rows), pl.ds(lane, value_width)] = (
                values(p, h)
            )
        return carry

    lax.fori_loop(0, half, keep_rows, 0)

    def place(i, carry):
        give_copy(i).wait()
        lane = pl.multiple_of((1 - role) * out_lanes, 128)
        out_ref[pl.ds(pl.multiple_of(i * pair_rows, 16), pair_rows), pl.ds(lane, out_lanes)] = taken[i]
        return carry

    lax.fori_loop(0, half, place, 0)

    def drain(step, carry):
        peer = lax.rem(me + step, shards)
        k_copy(step, peer, me).wait_send()
        r_copy(step, peer, me).wait_send()
        q_copy(step, peer, me).wait_send()
        rot_copy(step, peer, me).wait_send()
        for j in range(requests):
            back_copy(j, step, peer, me).wait_send()
        return carry

    lax.fori_loop(1, shards, drain, 0)


def body(
    states,
    w_latent,
    w_rope,
    latent_gain,
    span_len,
    cache_len,
    dest,
    page_table,
    latent_pool,
    rope_pool,
    new_keys,
    q_nope,
    q_rope,
    w_uk,
    w_uv,
):
    roles = lax.axis_size("role")
    shards = lax.axis_size("shard")
    tokens = states.shape[0]
    depth, width = w_latent.shape
    rope_width = w_rope.shape[1]
    requests = dest.shape[1]
    request_count = shards * requests
    pages, page_rows, _ = latent_pool.shape
    slot_cap, steps = new_keys.shape[1:3]
    heads_local, head_width, _ = w_uk.shape
    value_width = w_uv.shape[2]
    pages_each = pages // slot_cap
    heads = heads_local // roles
    assert roles == 2 and pages_each * page_rows - tokens // 2 == roles * page_rows
    each = steps * heads
    pair_rows = requests * steps
    half = shards // 2
    bf16, f32 = jnp.bfloat16, jnp.float32

    half_width = rope_width // 2
    frequency = 10000.0 ** (-jnp.arange(half_width, dtype=f32) / half_width)
    frequency = jnp.concatenate([frequency, frequency])[None, :]
    nope = jnp.swapaxes(q_nope, 0, 1).reshape(request_count * steps, -1)
    rotary = jnp.swapaxes(q_rope, 0, 1).reshape(shards, pair_rows, -1)
    recent = jnp.pad(new_keys[0], ((0, 0), (0, 16 - steps), (0, 128 - rope_width)))
    new_latent, new_rope = recent[:, :, :width], recent[:, :, width:]

    smem = pl.BlockSpec(memory_space=pltpu.SMEM)
    vmem = pl.BlockSpec(memory_space=pltpu.VMEM)
    anywhere = pl.BlockSpec(memory_space=pl.ANY)
    dims = (
        shards, requests, steps, heads, (head_width + rope_width) ** (-0.5), pages_each
    )
    sem = pltpu.SemaphoreType.DMA
    out = pl.pallas_call(
        functools.partial(kernel, dims),
        out_shape=jax.ShapeDtypeStruct((half * pair_rows, heads_local * value_width), bf16),
        in_specs=[smem] * 4 + [vmem] * 2 + [anywhere] * 11,
        out_specs=vmem,
        scratch_shapes=[
            pltpu.VMEM((tokens, depth), bf16),
            pltpu.VMEM((depth, width), bf16),
            pltpu.VMEM((depth, rope_width), bf16),
            pltpu.VMEM(latent_pool.shape, bf16),
            pltpu.VMEM(rope_pool.shape, bf16),
            pltpu.VMEM(new_latent.shape, bf16),
            pltpu.VMEM(new_rope.shape, bf16),
            pltpu.VMEM((request_count * steps, heads * head_width), bf16),
            pltpu.VMEM((heads * head_width, width), bf16),
            pltpu.VMEM((heads, width, value_width), bf16),
            pltpu.SMEM((shards,), jnp.int32),
            pltpu.VMEM((shards, page_rows + 16, width), bf16),
            pltpu.VMEM((shards, page_rows + 16, width), bf16),
            pltpu.VMEM((shards, rope_width + 16, 128), bf16),
            pltpu.VMEM((shards, rope_width + 16, 128), bf16),
            pltpu.VMEM((shards, requests, each, width), bf16),
            pltpu.VMEM((shards, requests, each, width), bf16),
            pltpu.VMEM((shards, pair_rows, heads * rope_width), bf16),
            pltpu.VMEM((shards, requests, each, rope_width), bf16),
            pltpu.VMEM((tokens, width), f32),
            pltpu.VMEM((tokens, rope_width), f32),
            pltpu.VMEM((tokens, width), f32),
            pltpu.VMEM((tokens, rope_width), f32),
            pltpu.VMEM((tokens, width), bf16),
            pltpu.VMEM((tokens, rope_width), bf16),
            pltpu.VMEM((requests, page_rows + 16, width), bf16),
            pltpu.VMEM((requests, rope_width + 16, 128), bf16),
            pltpu.VMEM((requests, page_rows, width), bf16),
            pltpu.VMEM((requests, rope_width, 128), bf16),
            pltpu.VMEM((requests, shards, each, width), bf16),
            pltpu.VMEM((shards, requests, each, width), bf16),
            pltpu.VMEM((half, pair_rows, heads * value_width), bf16),
            pltpu.VMEM((half, pair_rows, heads * value_width), bf16),
            sem((11,)),
            sem((2, shards)),
            sem((2, shards)),
            sem((2, shards)),
            sem((2, shards)),
            sem((2, 2)),
            sem((2, 2 * requests)),
            sem((2, requests, shards)),
            sem((2, half)),
        ],
        compiler_params=pltpu.CompilerParams(
            collective_id=0, has_side_effects=True, vmem_limit_bytes=56 * 1024 * 1024
        ),
    )(
        dest, cache_len, span_len, page_table, latent_gain[None, :], frequency,
        states, w_latent, w_rope, latent_pool, rope_pool, new_latent, new_rope, nope, rotary,
        w_uk.reshape(heads_local * head_width, width), w_uv,
    )
    return out.reshape(request_count // roles, steps, heads_local * value_width)


def solution(mesh):
    return jax.shard_map(
        body,
        mesh=mesh,
        in_specs=(
            P(("parts", "shard"), None),
            P("role", None),
            P("role", None),
            P(),
            P("parts", None),
            P("parts", None),
            P("parts", None),
            P(("parts", "shard"), None),
            P(("parts", "shard"), None, None),
            P(("parts", "shard"), None, None),
            P(("parts", "shard"), None, None, None),
            P(None, "parts", "shard"),
            P(None, "parts", "shard"),
            P("shard", None, None),
            P("shard", None, None),
        ),
        out_specs=P(("parts", "role"), None, "shard"),
        check_vma=False,
    )
```

profile of v0, /device:TPU:0, one launch (start us, length us, event | category | flops | bytes accessed | tf_op | source)
XLA Modules:
  0.0 114.9 jit_solution(1513050963803974127)
XLA Ops:
  0.0 0.0 copy-start
  0.0 0.7 maximum_bitcast_fusion.frequency_ref
  0.7 1.3 %broadcast_in_dim.6.gain_ref = bf16[1,512]{1,0:T(2,128)(2,1)} reshape(bf16[512]{0:T(512)(128)(2,1)} %param.18) | data formatting | bytes 2048 | tf_op jit(solution)/shard_map/broadcast_in_dim | solution.py:550
  1.9 1.3 %copy.20.span_ref = s32[8,4]{1,0:T(8,128)} copy(s32[8,4]{0,1:T(4,128)} %param.19) | data formatting | bytes 256 | tf_op args[4]
  3.3 1.3 %copy.19.cache_ref = s32[8,4]{1,0:T(8,128)} copy(s32[8,4]{0,1:T(4,128)} %param.20) | data formatting | bytes 256 | tf_op args[5]
  4.6 1.3 %copy.18.dest_ref = s32[8,4]{1,0:T(8,128)} copy(s32[8,4]{0,1:T(4,128)} %param.21) | data formatting | bytes 256 | tf_op args[6]
  6.0 1.3 %pad_slice_fusion.new_rope_hbm = bf16[8,16,128]{2,1,0:T(8,128)(2,1)} fusion(bf16[8,4,576]{2,1,0:T(4,128)(2,1)} %bitcast.9), kind=kLoop, calls=%fused_computation | loop fusion | bytes 69632 | tf_op jit(solution)/shard_map/slice | solution.py:488
  7.3 1.4 %pad_slice_fusion.1.new_latent_hbm = bf16[8,16,512]{2,1,0:T(8,128)(2,1)} fusion(bf16[8,4,576]{2,1,0:T(4,128)(2,1)} %bitcast.10), kind=kLoop, calls=%fused_computation.1 | loop fusion | bytes 167936 | tf_op jit(solution)/shard_map/slice | solution.py:488
  8.7 1.2 %copy.17 = bf16[32,4,1024]{2,1,0:T(4,128)(2,1)S(1)} copy(bf16[32,4,1024]{2,0,1:T(8,128)(2,1)} %bitcast.8) | data formatting | bytes 524288 | tf_op jit(solution)/shard_map/transpose | solution.py:486
  9.9 0.8 reshape.13.rotary_hbm
  10.6 1.4 %copy.16 = bf16[32,4,2048]{2,1,0:T(4,128)(2,1)S(1)} copy(bf16[32,4,2048]{2,0,1:T(8,128)(2,1)} %bitcast.7) | data formatting | bytes 1048576 | tf_op jit(solution)/shard_map/transpose | solution.py:485
  12.1 0.9 reshape.12.nope_hbm
  13.0 0.0 copy-done
  13.0 1.2 %copy.21.w_rope_hbm = bf16[3584,64]{1,0:T(8,128)(2,1)} copy(bf16[3584,64]{0,1:T(8,128)(2,1)S(1)} %copy-done) | data formatting | bytes 917504 | tf_op args[2]
  14.3 98.9 %shard_map.145 = bf16[64,2048]{1,0:T(8,128)(2,1)} custom-call(s32[8,4]{1,0:T(8,128)} %copy.18.dest_ref, s32[8,4]{1,0:T(8,128)} %copy.19.cache_ref, s32[8,4]{1,0:T(8,128)} %copy.20.span_ref, s32[1,24]{1,0:T(1,128)} %table_ref.1, bf16[1,512]{1,0:T(2,128)(2,1)} %broadcast_in_dim.6.gain_ref, f32[1,64]{1,0:T(1,128)} %maximum_bitcast_fusion.frequency_ref, ...), custom_call_target="tpu_custom_call" | custom-call | tf_op jit(solution)/shard_map/pallas_call | solution.py:497
  113.2 1.8 %reshape.15 = bf16[16,4,2048]{2,1,0:T(4,128)(2,1)} reshape(bf16[64,2048]{1,0:T(8,128)(2,1)} %shard_map.145) | data formatting | bytes 524288 | tf_op jit(solution)/shard_map/reshape | solution.py:554
  (1 shorter events, 0.0 us)
Async XLA Ops:
  0.0 13.0 %copy-start = (bf16[3584,64]{0,1:T(8,128)(2,1)S(1)}, bf16[3584,64]{0,1:T(8,128)(2,1)}, u32[]{:S(2)}) copy-start(bf16[3584,64]{0,1:T(8,128)(2,1)} %param.17) | copy-start | bytes 1376260
where the time goes:
time: 115 us
  Pallas kernels  98.9 us (86%)
  local copies, waits for them, and re-layouts  15.3 us (13%)
    pallas_call x1, Pallas kernels, body(): pl.pallas_call(functools.partial(kernel, dims), out_shape=jax.ShapeDtypeS...  98.9 us
    unnamed x6, local copies, waits for them, and re-layouts  5.28 us
    slice x2, local copies, waits for them, and re-layouts, body(): new_latent, new_rope = (recent[:, :, :width], recent[:, :, width:])  2.75 us

commit v1 on v0

--- a/solution.py
+++ b/solution.py
@@ -1,4 +1,5 @@
 import functools
+import math
 
 import jax
 import jax.numpy as jnp
@@ -36,14 +37,12 @@
     span_ref,
     table_ref,
     gain_ref,
-    frequency_ref,
     states_hbm,
     w_latent_hbm,
     w_rope_hbm,
     pool_hbm,
     rope_pool_hbm,
-    new_latent_hbm,
-    new_rope_hbm,
+    new_keys_hbm,
     nope_hbm,
     rotary_hbm,
     uk_hbm,
@@ -54,11 +53,12 @@
     w_rope,
     pool,
     rope_pool,
-    new_latent,
-    new_rope,
+    new_keys,
     nope,
+    rotary,
     uk,
     uv,
+    uv_wide,
     slots,
     k_send,
     k_got,
@@ -66,6 +66,7 @@
     r_got,
     q_send,
     q_got,
+    rotary_send,
     rotary_got,
     rotary_rows,
     part_latent,
@@ -97,7 +98,7 @@
     me = lax.axis_index("shard")
     bf16 = jnp.bfloat16
     page_rows, width = pool.shape[1:]
-    rope_width = w_rope.shape[1]
+    rope_width = w_rope.shape[0]
     depth = w_latent.shape[0]
     head_width = uk.shape[0] // heads
     value_width = uv.shape[2]
@@ -107,26 +108,24 @@
     half = shards // 2
     pair_rows = requests * steps
 
+    def own_lanes_of(source, target):
+        lanes = target.shape[-1]
+        return source.at[:, :, pl.ds(pl.multiple_of(role * lanes, 128), lanes)]
+
     loads = [
         (pool_hbm, pool),
         (rope_pool_hbm, rope_pool),
-        (new_latent_hbm, new_latent),
-        (new_rope_hbm, new_rope),
-        (nope_hbm.at[:, pl.ds(pl.multiple_of(role * nope.shape[1], 128), nope.shape[1])], nope),
+        (new_keys_hbm.at[0], new_keys),
+        (own_lanes_of(nope_hbm, nope), nope),
+        (own_lanes_of(rotary_hbm, rotary), rotary),
         (uk_hbm.at[pl.ds(pl.multiple_of(role * uk.shape[0], 128), uk.shape[0])], uk),
         (states_hbm.at[:, pl.ds(pl.multiple_of(role * depth, 128), depth)], states),
         (w_latent_hbm, w_latent),
         (w_rope_hbm, w_rope),
         (uv_hbm.at[pl.ds(role * heads, heads)], uv),
-        (
-            rotary_hbm.at[
-                me, :, pl.ds(pl.multiple_of(role * rotary_got.shape[2], 128), rotary_got.shape[2])
-            ],
-            rotary_got.at[me],
-        ),
     ]
     loads = [pltpu.make_async_copy(a, b, load_sem.at[i]) for i, (a, b) in enumerate(loads)]
-    for load in loads:
+    for load in loads[:6]:
         load.start()
 
     barrier = pltpu.get_barrier_semaphore()
@@ -158,14 +157,14 @@
     def find(p, count):
         slot = jnp.int32(0)
         for j in range(requests):
-            hit = dest_ref[p, j] == me
+            hit = dest_ref[j, p] == me
             slot = jnp.where(hit, count, slot)
             count = count + jnp.where(hit, 1, 0)
-        slots[p] = jnp.minimum(slot, new_latent.shape[0] - 1)
+        slots[p] = jnp.minimum(slot, new_keys.shape[0] - 1)
         return count
 
     lax.fori_loop(0, shards, find, jnp.int32(0))
-    for load in loads[:4]:
+    for load in loads[:3]:
         load.wait()
     pl.semaphore_wait(barrier, shards)
 
@@ -179,17 +178,19 @@
         return to_shard(q_send.at[peer], q_got.at[slot], q_sem, (step,), peer)
 
     def rot_copy(step, peer, slot):
-        lanes = rotary_got.shape[2]
-        source = rotary_hbm.at[peer, :, pl.ds(pl.multiple_of(role * lanes, 128), lanes)]
-        return to_shard(source, rotary_got.at[slot], rot_sem, (step,), peer)
+        return to_shard(rotary_send.at[peer], rotary_got.at[slot], rot_sem, (step,), peer)
 
     def fill_pages(latent_to, rope_to, peer):
         slot = slots[peer]
         page = table_ref[0, slot * pages_each + role]
-        latent_to[:page_rows] = pool[page]
-        latent_to[page_rows:] = new_latent[slot]
+        latent_to[...] = pool[page]
         rope_to[:rope_width] = rope_pool[page]
-        rope_to[rope_width:] = new_rope[slot]
+        recent = new_keys[slot]
+        blank = jnp.zeros((steps, 128 - rope_width), bf16)
+        pieces = [recent[:, c * 128 : (c + 1) * 128] for c in range(width // 128)]
+        pieces.append(jnp.concatenate([recent[:, width:], blank], axis=1))
+        pieces.append(jnp.zeros((rope_to.shape[0] - rope_width - steps * len(pieces), 128), bf16))
+        rope_to[rope_width:] = jnp.concatenate(pieces, axis=0)
 
     def send_pages(step, carry):
         peer = lax.rem(me + step, shards)
@@ -199,9 +200,15 @@
         return carry
 
     lax.fori_loop(1, shards, send_pages, 0)
-    for load in loads[4:6]:
+    for load in loads[3:6]:
         load.wait()
-
+    for load in loads[6:]:
+        load.start()
+
+    request_count = shards * requests
+    all_rows = steps * request_count
+    pair = (pair_rows, all_rows)
+    pair_source = lax.rem(iota(pair, 0), steps) * request_count + lax.div(iota(pair, 0), steps)
     spread = one_hot(
         lax.div(iota((query_rows, pair_rows), 0), heads) == iota((query_rows, pair_rows), 1)
     )
@@ -209,19 +216,21 @@
     own_lanes = lax.div(iota(shape, 1), head_width) == lax.rem(iota(shape, 0), heads)
 
     def absorb(peer):
-        rows = nope[pl.ds(pl.multiple_of(peer * pair_rows, 16), pair_rows), :]
+        pick = one_hot(iota(pair, 1) == pair_source + peer * requests)
+        rows = dot(pick, nope[...].reshape(all_rows, heads * head_width)).astype(bf16)
+        rotary_rows_of = dot(pick, rotary[...].reshape(all_rows, heads * rope_width)).astype(bf16)
         wide = jnp.where(own_lanes, dot(spread, rows), 0.0).astype(bf16)
-        return dot(wide, uk[...]).astype(bf16).reshape(requests, each, width)
+        return dot(wide, uk[...]).astype(bf16).reshape(requests, each, width), rotary_rows_of
 
     def send_queries(step, carry):
         peer = lax.rem(me + step, shards)
-        q_send[peer] = absorb(peer)
+        q_send[peer], rotary_send[peer] = absorb(peer)
         q_copy(step, peer, me).start()
         rot_copy(step, peer, me).start()
         return carry
 
     lax.fori_loop(1, shards, send_queries, 0)
-    q_got[me] = absorb(me)
+    q_got[me], rotary_got[me] = absorb(me)
     fill_pages(k_got.at[me], r_got.at[me], me)
 
     for load in loads[6:9]:
@@ -233,7 +242,7 @@
         where = pl.ds(pl.multiple_of(k * CHUNK, CHUNK), CHUNK)
         rows = states[:, where]
         part_latent[...] += dot(rows, w_latent[where, :])
-        part_rope[...] += dot(rows, w_rope[where, :])
+        part_rope[...] += dot_last(rows, w_rope[:, where])
         return carry
 
     lax.fori_loop(0, depth // CHUNK, project, 0)
@@ -248,10 +257,12 @@
     ends = jnp.int32(0)
     for j in range(requests):
         begin = ends
-        ends = ends + span_ref[me, j]
+        ends = ends + span_ref[j, me]
         inside = (row >= begin) & (row < ends)
-        position = position + jnp.where(inside, cache_ref[me, j] - begin, 0)
-    angle = position.astype(jnp.float32) * frequency_ref[...]
+        position = position + jnp.where(inside, cache_ref[j, me] - begin, 0)
+    rank = lax.rem(iota((1, rope_width), 1), rope_width // 2).astype(jnp.float32)
+    frequency = jnp.exp(rank * (-math.log(10000.0) / (rope_width // 2)))
+    angle = position.astype(jnp.float32) * frequency
     first = iota((tokens, rope_width), 1) < rope_width // 2
     cosine = jnp.cos(angle)
     sine = jnp.sin(angle)
@@ -261,12 +272,16 @@
     raw = part_latent[...] + there_latent[...]
     mean_square = jnp.sum(raw * raw, axis=1, keepdims=True) * (1.0 / width)
     span_latent[...] = (
-        raw * lax.rsqrt(mean_square + 1e-06) * gain_ref[...].astype(jnp.float32)
+        raw * lax.rsqrt(mean_square + 1e-06) * gain_ref[...].astype(jnp.float32).reshape(1, width)
     ).astype(bf16)
     raw = part_rope[...] + there_rope[...]
     turned = jnp.concatenate([raw[:, rope_width // 2 :], raw[:, : rope_width // 2]], axis=1)
     span_rope[...] = (raw * cosine + turned * sine).astype(bf16)
 
+    loads[9].wait()
+    for h in range(heads):
+        uv_wide[:, h * value_width : (h + 1) * value_width] = uv[h]
+
     def take_pages(step, carry):
         origin = lax.rem(me + shards - step, shards)
         k_copy(step, origin, origin).wait_recv()
@@ -276,11 +291,11 @@
     lax.fori_loop(1, shards, take_pages, 0)
     page_copies = []
     for j in range(requests):
-        mine_latent[j] = k_got[dest_ref[me, j]]
-        mine_rope[j] = r_got[dest_ref[me, j]]
+        mine_latent[j] = k_got[dest_ref[j, me]]
+        mine_rope[j] = r_got[dest_ref[j, me]]
     for j in range(requests):
         page_copies.append(
-            to_role(mine_latent.at[j, pl.ds(0, page_rows)], other_latent.at[j], page_sem, 2 * j)
+            to_role(mine_latent.at[j], other_latent.at[j], page_sem, 2 * j)
         )
         page_copies.append(
             to_role(mine_rope.at[j, pl.ds(0, rope_width)], other_rope.at[j], page_sem, 2 * j + 1)
@@ -288,7 +303,6 @@
     for copy in page_copies:
         copy.start()
 
-    loads[10].wait()
     lanes = heads * rope_width
     own_rope = lax.div(iota((query_rows, lanes), 1), rope_width) == lax.rem(
         iota((query_rows, lanes), 0), heads
@@ -322,14 +336,20 @@
     def attend(j, carry):
         begin = jnp.int32(0)
         for i in range(requests):
-            begin = begin + jnp.where(i < j, span_ref[me, i], 0)
-        end = begin + span_ref[me, j]
-        cached = cache_ref[me, j]
+            begin = begin + jnp.where(i < j, span_ref[i, me], 0)
+        end = begin + span_ref[j, me]
+        cached = cache_ref[j, me]
         ql = q_got[:, j].reshape(rows, width)
         qr = rotary_rows[:, j].reshape(rows, rope_width)
-        mine = mine_latent[j, :page_rows]
-        fresh = mine_latent[j, page_rows:]
-        fresh_rope = mine_rope[j, rope_width:, :rope_width]
+        mine = mine_latent[j]
+        recent = mine_rope[j, rope_width:]
+        chunks = width // 128
+        fresh = jnp.concatenate([recent[c * steps : (c + 1) * steps] for c in range(chunks)], axis=1)
+        fresh = jnp.concatenate([fresh, jnp.zeros((16 - steps, width), bf16)], axis=0)
+        fresh_rope = recent[chunks * steps : chunks * steps + steps, :rope_width]
+        fresh_rope = jnp.concatenate(
+            [fresh_rope, jnp.zeros((16 - steps, rope_width), bf16)], axis=0
+        )
         other = other_latent[j]
         page_column = iota((rows, page_rows), 1)
         span_column = iota((rows, tokens), 1)
@@ -379,7 +399,6 @@
         return carry
 
     lax.fori_loop(0, requests, attend, 0)
-    loads[9].wait()
 
     def arrived(p):
         step = lax.rem(me - p + shards, shards)
@@ -389,12 +408,17 @@
             for j in range(requests):
                 back_copy(j, step, p, p).wait_recv()
 
-    def values(p, h):
+    out_lanes = heads * value_width
+    wide_shape = (query_rows, out_lanes)
+    head_lanes = lax.div(iota(wide_shape, 1), value_width) == lax.rem(iota(wide_shape, 0), heads)
+    gather = one_hot(
+        lax.div(iota((pair_rows, query_rows), 1), heads) == iota((pair_rows, query_rows), 0)
+    )
+
+    def values(p):
         own = back[p].reshape(query_rows, width)
-        pick = one_hot(
-            iota((pair_rows, query_rows), 1) == iota((pair_rows, query_rows), 0) * heads + h
-        )
-        return dot(pick, dot(own, uv[h]).astype(bf16)).astype(bf16)
+        wide = jnp.where(head_lanes, dot(own, uv_wide[...]), 0.0).astype(bf16)
+        return dot(gather, wide).astype(bf16)
 
     def give_copy(i):
         return to_role(give.at[i], taken.at[i], give_sem, i)
@@ -402,22 +426,17 @@
     def give_rows(i, carry):
         p = (1 - role) * half + i
         arrived(p)
-        for h in range(heads):
-            give[i, :, h * value_width : (h + 1) * value_width] = values(p, h)
+        give[i] = values(p)
         give_copy(i).start()
         return carry
 
     lax.fori_loop(0, half, give_rows, 0)
-    out_lanes = heads * value_width
 
     def keep_rows(i, carry):
         p = role * half + i
         arrived(p)
-        for h in range(heads):
-            lane = pl.multiple_of(role * out_lanes + h * value_width, 128)
-            out_ref[pl.ds(pl.multiple_of(i * pair_rows, 16), pair_rows), pl.ds(lane, value_width)] = (
-                values(p, h)
-            )
+        lane = pl.multiple_of(role * out_lanes, 128)
+        out_ref[pl.ds(pl.multiple_of(i * pair_rows, 16), pair_rows), pl.ds(lane, out_lanes)] = values(p)
         return carry
 
     lax.fori_loop(0, half, keep_rows, 0)
@@ -479,14 +498,6 @@
     half = shards // 2
     bf16, f32 = jnp.bfloat16, jnp.float32
 
-    half_width = rope_width // 2
-    frequency = 10000.0 ** (-jnp.arange(half_width, dtype=f32) / half_width)
-    frequency = jnp.concatenate([frequency, frequency])[None, :]
-    nope = jnp.swapaxes(q_nope, 0, 1).reshape(request_count * steps, -1)
-    rotary = jnp.swapaxes(q_rope, 0, 1).reshape(shards, pair_rows, -1)
-    recent = jnp.pad(new_keys[0], ((0, 0), (0, 16 - steps), (0, 128 - rope_width)))
-    new_latent, new_rope = recent[:, :, :width], recent[:, :, width:]
-
     smem = pl.BlockSpec(memory_space=pltpu.SMEM)
     vmem = pl.BlockSpec(memory_space=pltpu.VMEM)
     anywhere = pl.BlockSpec(memory_space=pl.ANY)
@@ -494,29 +505,32 @@
         shards, requests, steps, heads, (head_width + rope_width) ** (-0.5), pages_each
     )
     sem = pltpu.SemaphoreType.DMA
+    tail = -(-(steps * (width // 128 + 1)) // 16) * 16
     out = pl.pallas_call(
         functools.partial(kernel, dims),
         out_shape=jax.ShapeDtypeStruct((half * pair_rows, heads_local * value_width), bf16),
-        in_specs=[smem] * 4 + [vmem] * 2 + [anywhere] * 11,
+        in_specs=[smem] * 4 + [vmem] + [anywhere] * 10,
         out_specs=vmem,
         scratch_shapes=[
             pltpu.VMEM((tokens, depth), bf16),
             pltpu.VMEM((depth, width), bf16),
-            pltpu.VMEM((depth, rope_width), bf16),
+            pltpu.VMEM((rope_width, depth), bf16),
             pltpu.VMEM(latent_pool.shape, bf16),
             pltpu.VMEM(rope_pool.shape, bf16),
-            pltpu.VMEM(new_latent.shape, bf16),
-            pltpu.VMEM(new_rope.shape, bf16),
-            pltpu.VMEM((request_count * steps, heads * head_width), bf16),
+            pltpu.VMEM(new_keys.shape[1:], bf16),
+            pltpu.VMEM((steps, request_count, heads * head_width), bf16),
+            pltpu.VMEM((steps, request_count, heads * rope_width), bf16),
             pltpu.VMEM((heads * head_width, width), bf16),
             pltpu.VMEM((heads, width, value_width), bf16),
+            pltpu.VMEM((width, heads * value_width), bf16),
             pltpu.SMEM((shards,), jnp.int32),
-            pltpu.VMEM((shards, page_rows + 16, width), bf16),
-            pltpu.VMEM((shards, page_rows + 16, width), bf16),
-            pltpu.VMEM((shards, rope_width + 16, 128), bf16),
-            pltpu.VMEM((shards, rope_width + 16, 128), bf16),
+            pltpu.VMEM((shards, page_rows, width), bf16),
+            pltpu.VMEM((shards, page_rows, width), bf16),
+            pltpu.VMEM((shards, rope_width + tail, 128), bf16),
+            pltpu.VMEM((shards, rope_width + tail, 128), bf16),
             pltpu.VMEM((shards, requests, each, width), bf16),
             pltpu.VMEM((shards, requests, each, width), bf16),
+            pltpu.VMEM((shards, pair_rows, heads * rope_width), bf16),
             pltpu.VMEM((shards, pair_rows, heads * rope_width), bf16),
             pltpu.VMEM((shards, requests, each, rope_width), bf16),
             pltpu.VMEM((tokens, width), f32),
@@ -525,15 +539,15 @@
             pltpu.VMEM((tokens, rope_width), f32),
             pltpu.VMEM((tokens, width), bf16),
             pltpu.VMEM((tokens, rope_width), bf16),
-            pltpu.VMEM((requests, page_rows + 16, width), bf16),
-            pltpu.VMEM((requests, rope_width + 16, 128), bf16),
+            pltpu.VMEM((requests, page_rows, width), bf16),
+            pltpu.VMEM((requests, rope_width + tail, 128), bf16),
             pltpu.VMEM((requests, page_rows, width), bf16),
             pltpu.VMEM((requests, rope_width, 128), bf16),
             pltpu.VMEM((requests, shards, each, width), bf16),
             pltpu.VMEM((shards, requests, each, width), bf16),
             pltpu.VMEM((half, pair_rows, heads * value_width), bf16),
             pltpu.VMEM((half, pair_rows, heads * value_width), bf16),
-            sem((11,)),
+            sem((10,)),
             sem((2, shards)),
             sem((2, shards)),
             sem((2, shards)),
@@ -547,8 +561,8 @@
             collective_id=0, has_side_effects=True, vmem_limit_bytes=56 * 1024 * 1024
         ),
     )(
-        dest, cache_len, span_len, page_table, latent_gain[None, :], frequency,
-        states, w_latent, w_rope, latent_pool, rope_pool, new_latent, new_rope, nope, rotary,
+        dest.T, cache_len.T, span_len.T, page_table, latent_gain,
+        states, w_latent, w_rope.T, latent_pool, rope_pool, new_keys, q_nope, q_rope,
         w_uk.reshape(heads_local * head_width, width), w_uv,
     )
     return out.reshape(request_count // roles, steps, heads_local * value_width)

time: 115 us -> 93.4 us (0.81)
  local copies, waits for them, and re-layouts: 15.3 us -> 1.76 us
  Pallas kernels: 98.9 us -> 91.5 us
    pallas_call x1, Pallas kernels: 98.9 us -> 91.5 us  [body(): pl.pallas_call(functools.partial(kernel, dims), out_shape=jax.ShapeDtypeS...]
    unnamed x6 -> x0, local copies, waits for them, and re-layouts: 5.28 us -> none
    slice x2 -> x0, local copies, waits for them, and re-layouts: 2.75 us -> none  [body(): new_latent, new_rope = (recent[:, :, :width], recent[:, :, width:])]
    transpose x2 -> x0, local copies, waits for them, and re-layouts: 2.6 us -> none  [the longest x1 1.45 us: body(): nope = jnp.swapaxes(q_nope, 0, 1).reshape(request_count * steps, -1)]
    reshape x2 -> x0, local copies, waits for them, and re-layouts: 1.7 us -> none  [the longest x1 0.93 us: body(): nope = jnp.swapaxes(q_nope, 0, 1).reshape(request_count * steps, -1)]
    broadcast_in_dim x1 -> x0, local copies, waits for them, and re-layouts: 1.26 us -> none  [body(): latent_gain[None, :]]
where the time goes in v1:
time: 93.4 us; the launch traced here: 93.3 us
  Pallas kernels  91.5 us (98%)
  local copies, waits for them, and re-layouts  1.76 us (2%)
    pallas_call x1, Pallas kernels, body(): pl.pallas_call(functools.partial(kernel, dims), out_shape=jax.ShapeDtypeS...  91.5 us

profile of v1, /device:TPU:0, one launch (start us, length us, event | category | flops | bytes accessed | tf_op | source)
XLA Modules:
  0.0 93.3 jit_solution(10806297070287336113)
XLA Ops:
  0.0 91.5 %shard_map.145 = bf16[64,2048]{1,0:T(8,128)(2,1)} custom-call(s32[4,8]{1,0:T(4,128)} %bitcast.7, s32[4,8]{1,0:T(4,128)} %bitcast.8, s32[4,8]{1,0:T(4,128)} %bitcast.9, s32[1,24]{1,0:T(1,128)} %table_ref.1, bf16[512]{0:T(512)(128)(2,1)} %gain_ref.1, bf16[256,7168]{1,0:T(8,128)(2,1)} %states_hbm.1, bf16[3584,512]{1,0:T(8,128)(2,1)} %w_latent_hbm.1, ...), custom_call_target="tpu_custom_call" | custom-call | tf_op jit(solution)/shard_map/pallas_call | solution.py:509
  91.5 1.8 %reshape.7 = bf16[16,4,2048]{2,1,0:T(4,128)(2,1)} reshape(bf16[64,2048]{1,0:T(8,128)(2,1)} %shard_map.145) | data formatting | bytes 524288 | tf_op jit(solution)/shard_map/reshape | solution.py:568

commit v2 on v1

--- a/solution.py
+++ b/solution.py
@@ -28,6 +28,18 @@
 
 def one_hot(hit):
     return jnp.where(hit, 1.0, 0.0).astype(jnp.bfloat16)
+
+
+def far_first(shards, act):
+    middle = shards // 2
+
+    def pair(k, carry):
+        act(middle - k, 0)
+        act(middle + k, 0)
+        return carry
+
+    act(middle, 0)
+    lax.fori_loop(1, middle, pair, 0)
 
 
 def kernel(
@@ -199,7 +211,7 @@
         r_copy(step, peer, me).start()
         return carry
 
-    lax.fori_loop(1, shards, send_pages, 0)
+    far_first(shards, send_pages)
     for load in loads[3:6]:
         load.wait()
     for load in loads[6:]:
@@ -229,7 +241,7 @@
         rot_copy(step, peer, me).start()
         return carry
 
-    lax.fori_loop(1, shards, send_queries, 0)
+    far_first(shards, send_queries)
     q_got[me], rotary_got[me] = absorb(me)
     fill_pages(k_got.at[me], r_got.at[me], me)
 
@@ -324,7 +336,7 @@
         q_copy(step, origin, origin).wait_recv()
         return carry
 
-    lax.fori_loop(1, shards, take_queries, 0)
+    far_first(shards, take_queries)
     for copy in page_copies:
         copy.wait()
 
@@ -394,7 +406,7 @@
             back_copy(j, step, peer, me).start()
             return inner
 
-        lax.fori_loop(1, shards, send, 0)
+        far_first(shards, send)
         back[me, j] = attended[j, me]
         return carry
 

time: 93.4 us -> 89.5 us (0.958)
  Pallas kernels: 91.5 us -> 87.6 us
    pallas_call x1, Pallas kernels: 91.5 us -> 87.6 us  [body(): pl.pallas_call(functools.partial(kernel, dims), out_shape=jax.ShapeDtypeS...]
where the time goes in v2:
time: 89.5 us; the launch traced here: 89.4 us
  Pallas kernels  87.6 us (98%)
  local copies, waits for them, and re-layouts  1.76 us (2%)
    pallas_call x1, Pallas kernels, body(): pl.pallas_call(functools.partial(kernel, dims), out_shape=jax.ShapeDtypeS...  87.6 us

profile of v2, /device:TPU:0, one launch (start us, length us, event | category | flops | bytes accessed | tf_op | source)
XLA Modules:
  0.0 89.4 jit_solution(7082974550067584729)
XLA Ops:
  0.0 87.6 %shard_map.145 = bf16[64,2048]{1,0:T(8,128)(2,1)} custom-call(s32[4,8]{1,0:T(4,128)} %bitcast.7, s32[4,8]{1,0:T(4,128)} %bitcast.8, s32[4,8]{1,0:T(4,128)} %bitcast.9, s32[1,24]{1,0:T(1,128)} %table_ref.1, bf16[512]{0:T(512)(128)(2,1)} %gain_ref.1, bf16[256,7168]{1,0:T(8,128)(2,1)} %states_hbm.1, bf16[3584,512]{1,0:T(8,128)(2,1)} %w_latent_hbm.1, ...), custom_call_target="tpu_custom_call" | custom-call | tf_op jit(solution)/shard_map/pallas_call | solution.py:521
  87.6 1.8 %reshape.7 = bf16[16,4,2048]{2,1,0:T(4,128)(2,1)} reshape(bf16[64,2048]{1,0:T(8,128)(2,1)} %shard_map.145) | data formatting | bytes 524288 | tf_op jit(solution)/shard_map/reshape | solution.py:580
